TPU v7x, 32 devices: a whole 2x2x4 slice. The times are simulated.
32 devices in a mesh: tm: 4 (over z), space: 8 (over y, x, core).
Axes of the slice: x: 2, y: 2, z: 4, core: 2. Of those that a mesh axis runs over, the one named last changes fastest.
Arguments:
- states: float32 [4, 64, 64, 256], P('tm', 'space'), may hold values from -6 to 6
- conductivity: float32 [64, 64, 256], P('space'), may hold values from 0.4 to 1.6
Outputs:
- updated: float32 [4, 64, 64, 256], P('tm', 'space')
All inputs are finite; a program needn't handle non-finite values.
Results may differ from a plain program's by a relative error of at most 0.0001.
Values sent between devices are 32-bit elements; how exact they have to be, the bound alone decides.
A program may use at most 64 MiB of HBM per device.

v0:
```python
import jax
import jax.numpy as jnp
from jax import lax
from jax.sharding import PartitionSpec as P

FSTEPS = 4


fine_rate = 0.1
coarsen = 4


def with_halo(block, sides, width):
    for axis, dim in sides:
        count = lax.axis_size(axis)
        forward = [(i, i + 1) for i in range(count - 1)]
        backward = [(target, source) for source, target in forward]
        low = lax.ppermute(
            lax.slice_in_dim(block, block.shape[dim] - width, None, axis=dim), axis, forward
        )
        high = lax.ppermute(lax.slice_in_dim(block, 0, width, axis=dim), axis, backward)
        block = jnp.concatenate([low, block, high], axis=dim)
    return block


def passed_along(block, axis, distance):
    devices = range(lax.axis_size(axis))
    route = [(i - distance, i) for i in devices if i - distance in devices]
    return lax.ppermute(block, axis, route)


def plane_div(field, conduct, axis):
    count = field.shape[axis]
    upper = lax.slice_in_dim(field, 1, count, axis=axis)
    lower = lax.slice_in_dim(field, 0, count - 1, axis=axis)
    upper_c = lax.slice_in_dim(conduct, 1, count, axis=axis)
    lower_c = lax.slice_in_dim(conduct, 0, count - 1, axis=axis)
    flux = 0.5 * (upper_c + lower_c) * (upper - lower)
    widths = [(0, 0), (0, 0), (0, 0)]
    widths[axis] = (1, 1)
    padded = jnp.pad(flux, widths)
    return lax.slice_in_dim(padded, 1, count + 1, axis=axis) - lax.slice_in_dim(
        padded, 0, count, axis=axis
    )


def padded_step(padded, conduct, valid, step_rate):
    faces = valid[1:] * valid[:-1]
    flux_z = 0.5 * (conduct[1:] + conduct[:-1]) * (padded[1:] - padded[:-1]) * faces[:, None, None]
    div_z = flux_z[1:] - flux_z[:-1]
    centre = padded[1:-1]
    centre_c = conduct[1:-1]
    div_x = plane_div(centre, centre_c, 1)
    div_y = plane_div(centre, centre_c, 2)
    return centre + step_rate * (div_z + div_x + div_y)


def validity(planes, margin, local_planes):
    first = lax.axis_index("space") * local_planes - margin
    global_plane = first + jnp.arange(planes, dtype=jnp.int32)
    extent = lax.axis_size("space") * local_planes
    return ((global_plane >= 0) & (global_plane < extent)).astype(jnp.float32)


def restrict(field):
    planes, rows, cols = field.shape
    blocks = field.reshape(
        planes // coarsen, coarsen, rows // coarsen, coarsen, cols // coarsen, coarsen
    )
    return jnp.mean(blocks, axis=(1, 3, 5))


def prolong(coarse):
    return jnp.repeat(
        jnp.repeat(jnp.repeat(coarse, coarsen, axis=0), coarsen, axis=1), coarsen, axis=2
    )


def fine_run(field, conduct):
    local_planes = field.shape[0]
    padded = with_halo(field, (("space", 0),), FSTEPS)
    wide_conduct = with_halo(conduct, (("space", 0),), FSTEPS)
    valid = validity(local_planes + 2 * FSTEPS, FSTEPS, local_planes)
    for turn in range(FSTEPS):
        extent = padded.shape[0]
        padded = padded_step(
            padded, wide_conduct[turn : turn + extent], valid[turn : turn + extent], fine_rate
        )
    return padded


def per_device(states, conductivity):
    coarse_rate = fine_rate * FSTEPS / 16.0
    field = states[0]
    fine_end = fine_run(field, conductivity)
    coarse_conduct = restrict(conductivity)
    coarse_planes = coarse_conduct.shape[0]
    padded_conduct = with_halo(coarse_conduct, (("space", 0),), 1)
    coarse_valid = validity(coarse_planes + 2, 1, coarse_planes)

    def propagate(coarse):
        padded = with_halo(coarse, (("space", 0),), 1)
        return padded_step(padded, padded_conduct, coarse_valid, coarse_rate)

    coarse_first = restrict(field)
    coarse_old = propagate(coarse_first)
    jump = restrict(fine_end) - coarse_old
    position = lax.axis_index("tm")
    coarse_new = coarse_old
    carried = coarse_new + jump
    for rounds in range(lax.axis_size("tm") - 1):
        inbound = passed_along(carried, "tm", 1)
        start_state = jnp.where(position == 0, coarse_first, inbound)
        coarse_new = propagate(start_state)
        carried = coarse_new + jump
    result = fine_end + prolong(coarse_new - coarse_old)
    return result[None]


def solution(mesh):
    in_specs = (P("tm", "space", None, None), P("space", None, None))
    out_specs = P("tm", "space", None, None)
    return jax.shard_map(
        per_device, mesh=mesh, in_specs=in_specs, out_specs=out_specs, check_vma=False
    )
```

profile of v0, /device:TPU:27, one launch (start us, length us, event | category | flops | bytes accessed | tf_op | source)
XLA Modules:
  0.0 174.6 jit_solution(11602532469744497368)
XLA Ops:
  0.0 1.5 copy.53
  1.5 1.1 fusion.91
  2.7 3.7 %collective-permute-start.2 = (f32[4,64,256]{1,0,2:T(4,128)}, f32[4,64,256]{1,0,2:T(4,128)S(1)}, u32[]{:S(2)}, u32[]{:S(2)}) collective-permute-start(f32[4,64,256]{1,0,2:T(4,128)} %get-tuple-element.11), channel_id=1, source_target_pairs={{0,1},{1,2},{2,3},{3,4},{4,5},{5,6},{6,7},{8,9},{9,10},{10,11},{11... | collective-permute-start | bytes 786440 | tf_op jit(solution)/shard_map/ppermute | solution.py:18
  6.3 1.9 %collective-permute-start.3 = (f32[4,64,256]{1,0,2:T(4,128)}, f32[4,64,256]{1,0,2:T(4,128)}, u32[]{:S(2)}, u32[]{:S(2)}) collective-permute-start(f32[4,64,256]{1,0,2:T(4,128)} %get-tuple-element.12), channel_id=1, source_target_pairs={{1,0},{2,1},{3,2},{4,3},{5,4},{6,5},{7,6},{9,8},{10,9},{11,10},{12... | collective-permute-start | bytes 786440 | tf_op jit(solution)/shard_map/ppermute | solution.py:21
  8.3 18.6 %reshape_squeeze.3 = f32[2,4,16,4,64,4]{5,4,3,2,1,0:T(8,128)} reshape(f32[1,8,64,256]{3,2,1,0:T(8,128)S(1)} %copy-done.1) | data formatting | bytes 1048576 | tf_op jit(solution)/shard_map/reshape;squeeze | solution.py:67
  26.9 7.1 %reduce_sum.27 = f32[2,16,64]{2,1,0:T(8,128)S(1)} reduce(f32[2,4,16,4,64,4]{5,4,3,2,1,0:T(8,128)} %reshape_squeeze.3, f32[]{:T(128)} %constant.20.clone.1), dimensions={1,3,5}, to_apply=%region_0.1 | reduce | flops 129024 | bytes 532484 | tf_op jit(solution)/shard_map/reduce_sum | solution.py:70
  34.0 4.5 %collective-permute-start.7 = (f32[1,16,64]{2,1,0:T(8,128)S(1)}, f32[1,16,64]{2,1,0:T(8,128)S(1)}, u32[]{:S(2)}, u32[]{:S(2)}) collective-permute-start(f32[1,16,64]{2,1,0:T(8,128)S(1)} %get-tuple-element.23), channel_id=1, source_target_pairs={{0,1},{1,2},{2,3},{3,4},{4,5},{5,6},{6,7},{8,9},{9,10},{10,11},{11... | collective-permute-start | bytes 12296 | tf_op jit(solution)/shard_map/ppermute | solution.py:18
  38.6 1.9 %collective-permute-start.6 = (f32[1,16,64]{2,1,0:T(8,128)S(1)}, f32[1,16,64]{2,1,0:T(8,128)S(1)}, u32[]{:S(2)}, u32[]{:S(2)}) collective-permute-start(f32[1,16,64]{2,1,0:T(8,128)S(1)} %get-tuple-element.24), channel_id=1, source_target_pairs={{1,0},{2,1},{3,2},{4,3},{5,4},{6,5},{7,6},{9,8},{10,9},{11,10},{12... | collective-permute-start | bytes 12296 | tf_op jit(solution)/shard_map/ppermute | solution.py:21
  40.5 18.6 %reshape.22 = f32[2,4,16,4,64,4]{5,4,3,2,1,0:T(8,128)} reshape(f32[8,64,256]{2,1,0:T(8,128)S(1)} %copy-done) | data formatting | bytes 1048576 | tf_op jit(solution)/shard_map/reshape | solution.py:67
  59.2 7.0 %reduce_sum.28 = f32[2,16,64]{2,1,0:T(8,128)S(1)} reduce(f32[2,4,16,4,64,4]{5,4,3,2,1,0:T(8,128)} %reshape.22, f32[]{:T(128)} %constant.20.clone.1), dimensions={1,3,5}, to_apply=%region_1.2 | reduce | flops 129024 | bytes 532484 | tf_op jit(solution)/shard_map/reduce_sum | solution.py:70
  66.2 1.9 %collective-permute-start.4 = (f32[1,16,64]{2,1,0:T(8,128)S(1)}, f32[1,16,64]{2,1,0:T(8,128)S(1)}, u32[]{:S(2)}, u32[]{:S(2)}) collective-permute-start(f32[1,16,64]{2,1,0:T(8,128)S(1)} %get-tuple-element.21), channel_id=1, source_target_pairs={{1,0},{2,1},{3,2},{4,3},{5,4},{6,5},{7,6},{9,8},{10,9},{11,10},{12... | collective-permute-start | bytes 12296 | tf_op jit(solution)/shard_map/ppermute | solution.py:21
  69.0 1.0 slice_bitcast_fusion.1
  69.9 4.5 %collective-permute-start.5 = (f32[1,16,64]{2,1,0:T(8,128)S(1)}, f32[1,16,64]{2,1,0:T(8,128)S(1)}, u32[]{:S(2)}, u32[]{:S(2)}) collective-permute-start(f32[1,16,64]{2,1,0:T(8,128)S(1)} %get-tuple-element.22), channel_id=1, source_target_pairs={{0,1},{1,2},{2,3},{3,4},{4,5},{5,6},{6,7},{8,9},{9,10},{10,11},{11... | collective-permute-start | bytes 12296 | tf_op jit(solution)/shard_map/ppermute | solution.py:18
  74.6 2.4 %collective-permute-start = (f32[4,64,256]{1,0,2:T(4,128)}, f32[4,64,256]{1,0,2:T(4,128)S(1)}, u32[]{:S(2)}, u32[]{:S(2)}) collective-permute-start(f32[4,64,256]{1,0,2:T(4,128)} %get-tuple-element.13), channel_id=1, source_target_pairs={{0,1},{1,2},{2,3},{3,4},{4,5},{5,6},{6,7},{8,9},{9,10},{10,11},{11... | collective-permute-start | bytes 786440 | tf_op jit(solution)/shard_map/ppermute | solution.py:18
  77.0 2.1 %collective-permute-start.1 = (f32[4,64,256]{1,0,2:T(4,128)S(1)}, f32[4,64,256]{1,0,2:T(4,128)S(1)}, u32[]{:S(2)}, u32[]{:S(2)}) collective-permute-start(f32[4,64,256]{1,0,2:T(4,128)S(1)} %get-tuple-element.14), channel_id=1, source_target_pairs={{1,0},{2,1},{3,2},{4,3},{5,4},{6,5},{7,6},{9,8},{10,9},{11,10},{12... | collective-permute-start | bytes 786440 | tf_op jit(solution)/shard_map/ppermute | solution.py:21
  79.2 1.5 pad_maximum_fusion.3
  80.7 6.3 %collective-permute-done = f32[4,64,256]{1,0,2:T(4,128)S(1)} collective-permute-done((f32[4,64,256]{1,0,2:T(4,128)}, f32[4,64,256]{1,0,2:T(4,128)S(1)}, u32[]{:S(2)}, u32[]{:S(2)}) %collective-permute-start) | collective-permute-done | bytes 262176 | tf_op jit(solution)/shard_map/ppermute | solution.py:18
  87.0 2.0 %collective-permute-done.1 = f32[4,64,256]{1,0,2:T(4,128)S(1)} collective-permute-done((f32[4,64,256]{1,0,2:T(4,128)S(1)}, f32[4,64,256]{1,0,2:T(4,128)S(1)}, u32[]{:S(2)}, u32[]{:S(2)}) %collective-permute-start.1) | collective-permute-done | bytes 262176 | tf_op jit(solution)/shard_map/ppermute | solution.py:21
  90.0 1.1 fusion.22
  91.2 0.6 fusion.29
  91.8 1.4 fusion.27
  93.7 1.1 fusion.13
  94.8 0.8 fusion.20
  95.6 1.4 fusion.18
  97.5 1.1 fusion.4
  98.7 0.8 fusion.11
  99.4 1.6 fusion.9
  101.3 0.7 fusion.37
  101.9 2.0 %fusion.1 = f32[9,64,256]{1,0,2:T(8,128)S(1)} fusion(f32[10,64,256]{1,0,2:T(8,128)S(1)} %fusion.9, f32[8,64,256]{1,0,2:T(8,128)S(1)} %copy.53, f32[4,64,256]{1,0,2:T(4,128)S(1)} %collective-permute-done.2, f32[4,64,256]{1,0,2:T(4,128)} %collective-permute-done.3, f32[9]{0:T(128)S(1)} %slice_multiply_fusion.1), kind=kLoop, calls=%fused_computation.2 | loop fusion | flops 1032192 | bytes 2818084 | tf_op jit(solution)/shard_map/mul | solution.py:49
  104.0 0.7 fusion.42
  105.0 18.6 %reshape.23 = f32[2,4,16,4,64,4]{5,4,3,2,1,0:T(8,128)} reshape(f32[8,64,256]{2,1,0:T(8,128)S(1)} %copy.62) | data formatting | bytes 1048576 | tf_op jit(solution)/shard_map/reshape | solution.py:67
  123.6 7.0 %reduce_sum.29 = f32[2,16,64]{2,1,0:T(8,128)S(1)} reduce(f32[2,4,16,4,64,4]{5,4,3,2,1,0:T(8,128)} %reshape.23, f32[]{:T(128)} %constant.20.clone.1), dimensions={1,3,5}, to_apply=%region_2.3 | reduce | flops 129024 | bytes 532484 | tf_op jit(solution)/shard_map/reduce_sum | solution.py:70
  130.8 1.3 collective-permute-start.8
  132.1 3.2 %collective-permute-done.8 = f32[2,16,64]{2,1,0:T(8,128)S(1)} collective-permute-done((f32[2,16,64]{2,1,0:T(8,128)S(1)}, f32[2,16,64]{2,1,0:T(8,128)S(1)}, u32[]{:S(2)}, u32[]{:S(2)}) %collective-permute-start.8) | collective-permute-done | bytes 8224 | tf_op jit(solution)/shard_map/ppermute | solution.py:29
  135.3 4.4 %collective-permute-start.10 = (f32[1,16,64]{2,1,0:T(8,128)S(1)}, f32[1,16,64]{2,1,0:T(8,128)S(1)}, u32[]{:S(2)}, u32[]{:S(2)}) collective-permute-start(f32[1,16,64]{2,1,0:T(8,128)S(1)} %get-tuple-element.19), channel_id=1, source_target_pairs={{0,1},{1,2},{2,3},{3,4},{4,5},{5,6},{6,7},{8,9},{9,10},{10,11},{11... | collective-permute-start | bytes 12296 | tf_op jit(solution)/shard_map/ppermute | solution.py:18
  139.7 1.9 %collective-permute-start.9 = (f32[1,16,64]{2,1,0:T(8,128)S(1)}, f32[1,16,64]{2,1,0:T(8,128)S(1)}, u32[]{:S(2)}, u32[]{:S(2)}) collective-permute-start(f32[1,16,64]{2,1,0:T(8,128)S(1)} %get-tuple-element.20), channel_id=1, source_target_pairs={{1,0},{2,1},{3,2},{4,3},{5,4},{6,5},{7,6},{9,8},{10,9},{11,10},{12... | collective-permute-start | bytes 12296 | tf_op jit(solution)/shard_map/ppermute | solution.py:21
  141.7 3.9 %collective-permute-done.9 = f32[1,16,64]{2,1,0:T(8,128)S(1)} collective-permute-done((f32[1,16,64]{2,1,0:T(8,128)S(1)}, f32[1,16,64]{2,1,0:T(8,128)S(1)}, u32[]{:S(2)}, u32[]{:S(2)}) %collective-permute-start.9) | collective-permute-done | bytes 4128 | tf_op jit(solution)/shard_map/ppermute | solution.py:21
  145.7 1.3 collective-permute-start.11
  147.0 3.2 %collective-permute-done.11 = f32[2,16,64]{2,1,0:T(8,128)S(1)} collective-permute-done((f32[2,16,64]{2,1,0:T(8,128)S(1)}, f32[2,16,64]{2,1,0:T(8,128)S(1)}, u32[]{:S(2)}, u32[]{:S(2)}) %collective-permute-start.11) | collective-permute-done | bytes 8224 | tf_op jit(solution)/shard_map/ppermute | solution.py:29
  150.3 3.1 %collective-permute-start.13 = (f32[1,16,64]{2,1,0:T(8,128)S(1)}, f32[1,16,64]{2,1,0:T(8,128)S(1)}, u32[]{:S(2)}, u32[]{:S(2)}) collective-permute-start(f32[1,16,64]{2,1,0:T(8,128)S(1)} %get-tuple-element.17), channel_id=1, source_target_pairs={{0,1},{1,2},{2,3},{3,4},{4,5},{5,6},{6,7},{8,9},{9,10},{10,11},{11... | collective-permute-start | bytes 12296 | tf_op jit(solution)/shard_map/ppermute | solution.py:18
  153.4 1.9 %collective-permute-start.12 = (f32[1,16,64]{2,1,0:T(8,128)S(1)}, f32[1,16,64]{2,1,0:T(8,128)S(1)}, u32[]{:S(2)}, u32[]{:S(2)}) collective-permute-start(f32[1,16,64]{2,1,0:T(8,128)S(1)} %get-tuple-element.18), channel_id=1, source_target_pairs={{1,0},{2,1},{3,2},{4,3},{5,4},{6,5},{7,6},{9,8},{10,9},{11,10},{12... | collective-permute-start | bytes 12296 | tf_op jit(solution)/shard_map/ppermute | solution.py:21
  155.3 3.9 %collective-permute-done.12 = f32[1,16,64]{2,1,0:T(8,128)S(1)} collective-permute-done((f32[1,16,64]{2,1,0:T(8,128)S(1)}, f32[1,16,64]{2,1,0:T(8,128)S(1)}, u32[]{:S(2)}, u32[]{:S(2)}) %collective-permute-start.12) | collective-permute-done | bytes 4128 | tf_op jit(solution)/shard_map/ppermute | solution.py:21
  159.4 1.3 collective-permute-start.14
  160.7 3.2 %collective-permute-done.14 = f32[2,16,64]{2,1,0:T(8,128)S(1)} collective-permute-done((f32[2,16,64]{2,1,0:T(8,128)S(1)}, f32[2,16,64]{2,1,0:T(8,128)S(1)}, u32[]{:S(2)}, u32[]{:S(2)}) %collective-permute-start.14) | collective-permute-done | bytes 8224 | tf_op jit(solution)/shard_map/ppermute | solution.py:29
  164.0 3.1 %collective-permute-start.16 = (f32[1,16,64]{2,1,0:T(8,128)S(1)}, f32[1,16,64]{2,1,0:T(8,128)S(1)}, u32[]{:S(2)}, u32[]{:S(2)}) collective-permute-start(f32[1,16,64]{2,1,0:T(8,128)S(1)} %get-tuple-element.15), channel_id=1, source_target_pairs={{0,1},{1,2},{2,3},{3,4},{4,5},{5,6},{6,7},{8,9},{9,10},{10,11},{11... | collective-permute-start | bytes 12296 | tf_op jit(solution)/shard_map/ppermute | solution.py:18
  167.1 1.9 %collective-permute-start.15 = (f32[1,16,64]{2,1,0:T(8,128)S(1)}, f32[1,16,64]{2,1,0:T(8,128)S(1)}, u32[]{:S(2)}, u32[]{:S(2)}) collective-permute-start(f32[1,16,64]{2,1,0:T(8,128)S(1)} %get-tuple-element.16), channel_id=1, source_target_pairs={{1,0},{2,1},{3,2},{4,3},{5,4},{6,5},{7,6},{9,8},{10,9},{11,10},{12... | collective-permute-start | bytes 12296 | tf_op jit(solution)/shard_map/ppermute | solution.py:21
  169.0 3.9 %collective-permute-done.15 = f32[1,16,64]{2,1,0:T(8,128)S(1)} collective-permute-done((f32[1,16,64]{2,1,0:T(8,128)S(1)}, f32[1,16,64]{2,1,0:T(8,128)S(1)}, u32[]{:S(2)}, u32[]{:S(2)}) %collective-permute-start.15) | collective-permute-done | bytes 4128 | tf_op jit(solution)/shard_map/ppermute | solution.py:21
  173.4 1.2 copy.65
  (58 shorter events, 4.9 us)
Async XLA Ops:
  0.0 8.3 %copy-start.1 = (f32[1,8,64,256]{3,2,1,0:T(8,128)S(1)}, f32[1,8,64,256]{3,2,1,0:T(8,128)}, u32[]{:S(2)}) copy-start(f32[1,8,64,256]{3,2,1,0:T(8,128)} %param.2) | copy-start | bytes 1572868
  2.7 76.5 %collective-permute-start.2 = (f32[4,64,256]{1,0,2:T(4,128)}, f32[4,64,256]{1,0,2:T(4,128)S(1)}, u32[]{:S(2)}, u32[]{:S(2)}) collective-permute-start(f32[4,64,256]{1,0,2:T(4,128)} %get-tuple-element.11), channel_id=1, source_target_pairs={{0,1},{1,2},{2,3},{3,4},{4,5},{5,6},{6,7},{8,9},{9,10},{10,11},{11... | collective-permute-start | bytes 786440 | tf_op jit(solution)/shard_map/ppermute | solution.py:18
  6.3 72.8 %collective-permute-start.3 = (f32[4,64,256]{1,0,2:T(4,128)}, f32[4,64,256]{1,0,2:T(4,128)}, u32[]{:S(2)}, u32[]{:S(2)}) collective-permute-start(f32[4,64,256]{1,0,2:T(4,128)} %get-tuple-element.12), channel_id=1, source_target_pairs={{1,0},{2,1},{3,2},{4,3},{5,4},{6,5},{7,6},{9,8},{10,9},{11,10},{12... | collective-permute-start | bytes 786440 | tf_op jit(solution)/shard_map/ppermute | solution.py:21
  26.9 13.6 %copy-start = (f32[8,64,256]{2,1,0:T(8,128)S(1)}, f32[8,64,256]{2,1,0:T(8,128)}, u32[]{:S(2)}) copy-start(f32[8,64,256]{2,1,0:T(8,128)} %param.3) | copy-start | bytes 1572868
  34.0 35.9 %collective-permute-start.7 = (f32[1,16,64]{2,1,0:T(8,128)S(1)}, f32[1,16,64]{2,1,0:T(8,128)S(1)}, u32[]{:S(2)}, u32[]{:S(2)}) collective-permute-start(f32[1,16,64]{2,1,0:T(8,128)S(1)} %get-tuple-element.23), channel_id=1, source_target_pairs={{0,1},{1,2},{2,3},{3,4},{4,5},{5,6},{6,7},{8,9},{9,10},{10,11},{11... | collective-permute-start | bytes 12296 | tf_op jit(solution)/shard_map/ppermute | solution.py:18
  38.6 36.0 %collective-permute-start.6 = (f32[1,16,64]{2,1,0:T(8,128)S(1)}, f32[1,16,64]{2,1,0:T(8,128)S(1)}, u32[]{:S(2)}, u32[]{:S(2)}) collective-permute-start(f32[1,16,64]{2,1,0:T(8,128)S(1)} %get-tuple-element.24), channel_id=1, source_target_pairs={{1,0},{2,1},{3,2},{4,3},{5,4},{6,5},{7,6},{9,8},{10,9},{11,10},{12... | collective-permute-start | bytes 12296 | tf_op jit(solution)/shard_map/ppermute | solution.py:21
  66.2 10.7 %collective-permute-start.4 = (f32[1,16,64]{2,1,0:T(8,128)S(1)}, f32[1,16,64]{2,1,0:T(8,128)S(1)}, u32[]{:S(2)}, u32[]{:S(2)}) collective-permute-start(f32[1,16,64]{2,1,0:T(8,128)S(1)} %get-tuple-element.21), channel_id=1, source_target_pairs={{1,0},{2,1},{3,2},{4,3},{5,4},{6,5},{7,6},{9,8},{10,9},{11,10},{12... | collective-permute-start | bytes 12296 | tf_op jit(solution)/shard_map/ppermute | solution.py:21
  69.9 9.1 %collective-permute-start.5 = (f32[1,16,64]{2,1,0:T(8,128)S(1)}, f32[1,16,64]{2,1,0:T(8,128)S(1)}, u32[]{:S(2)}, u32[]{:S(2)}) collective-permute-start(f32[1,16,64]{2,1,0:T(8,128)S(1)} %get-tuple-element.22), channel_id=1, source_target_pairs={{0,1},{1,2},{2,3},{3,4},{4,5},{5,6},{6,7},{8,9},{9,10},{10,11},{11... | collective-permute-start | bytes 12296 | tf_op jit(solution)/shard_map/ppermute | solution.py:18
  74.6 12.4 %collective-permute-start = (f32[4,64,256]{1,0,2:T(4,128)}, f32[4,64,256]{1,0,2:T(4,128)S(1)}, u32[]{:S(2)}, u32[]{:S(2)}) collective-permute-start(f32[4,64,256]{1,0,2:T(4,128)} %get-tuple-element.13), channel_id=1, source_target_pairs={{0,1},{1,2},{2,3},{3,4},{4,5},{5,6},{6,7},{8,9},{9,10},{10,11},{11... | collective-permute-start | bytes 786440 | tf_op jit(solution)/shard_map/ppermute | solution.py:18
  77.0 12.0 %collective-permute-start.1 = (f32[4,64,256]{1,0,2:T(4,128)S(1)}, f32[4,64,256]{1,0,2:T(4,128)S(1)}, u32[]{:S(2)}, u32[]{:S(2)}) collective-permute-start(f32[4,64,256]{1,0,2:T(4,128)S(1)} %get-tuple-element.14), channel_id=1, source_target_pairs={{1,0},{2,1},{3,2},{4,3},{5,4},{6,5},{7,6},{9,8},{10,9},{11,10},{12... | collective-permute-start | bytes 786440 | tf_op jit(solution)/shard_map/ppermute | solution.py:21
  130.8 4.5 %collective-permute-start.8 = (f32[2,16,64]{2,1,0:T(8,128)S(1)}, f32[2,16,64]{2,1,0:T(8,128)S(1)}, u32[]{:S(2)}, u32[]{:S(2)}) collective-permute-start(f32[2,16,64]{2,1,0:T(8,128)S(1)} %get-tuple-element.5), channel_id=1, source_target_pairs={{0,8},{8,16},{16,24},{1,9},{9,17},{17,25},{2,10},{10,18},{18,26},{... | collective-permute-start | bytes 24584 | tf_op jit(solution)/shard_map/ppermute | solution.py:29
  135.3 6.3 %collective-permute-start.10 = (f32[1,16,64]{2,1,0:T(8,128)S(1)}, f32[1,16,64]{2,1,0:T(8,128)S(1)}, u32[]{:S(2)}, u32[]{:S(2)}) collective-permute-start(f32[1,16,64]{2,1,0:T(8,128)S(1)} %get-tuple-element.19), channel_id=1, source_target_pairs={{0,1},{1,2},{2,3},{3,4},{4,5},{5,6},{6,7},{8,9},{9,10},{10,11},{11... | collective-permute-start | bytes 12296 | tf_op jit(solution)/shard_map/ppermute | solution.py:18
  139.7 5.9 %collective-permute-start.9 = (f32[1,16,64]{2,1,0:T(8,128)S(1)}, f32[1,16,64]{2,1,0:T(8,128)S(1)}, u32[]{:S(2)}, u32[]{:S(2)}) collective-permute-start(f32[1,16,64]{2,1,0:T(8,128)S(1)} %get-tuple-element.20), channel_id=1, source_target_pairs={{1,0},{2,1},{3,2},{4,3},{5,4},{6,5},{7,6},{9,8},{10,9},{11,10},{12... | collective-permute-start | bytes 12296 | tf_op jit(solution)/shard_map/ppermute | solution.py:21
  145.7 4.5 %collective-permute-start.11 = (f32[2,16,64]{2,1,0:T(8,128)S(1)}, f32[2,16,64]{2,1,0:T(8,128)S(1)}, u32[]{:S(2)}, u32[]{:S(2)}) collective-permute-start(f32[2,16,64]{2,1,0:T(8,128)S(1)} %fusion.64), channel_id=1, source_target_pairs={{0,8},{8,16},{16,24},{1,9},{9,17},{17,25},{2,10},{10,18},{18,26},{... | collective-permute-start | bytes 24584 | tf_op jit(solution)/shard_map/ppermute | solution.py:29
  150.3 5.0 %collective-permute-start.13 = (f32[1,16,64]{2,1,0:T(8,128)S(1)}, f32[1,16,64]{2,1,0:T(8,128)S(1)}, u32[]{:S(2)}, u32[]{:S(2)}) collective-permute-start(f32[1,16,64]{2,1,0:T(8,128)S(1)} %get-tuple-element.17), channel_id=1, source_target_pairs={{0,1},{1,2},{2,3},{3,4},{4,5},{5,6},{6,7},{8,9},{9,10},{10,11},{11... | collective-permute-start | bytes 12296 | tf_op jit(solution)/shard_map/ppermute | solution.py:18
  153.4 5.9 %collective-permute-start.12 = (f32[1,16,64]{2,1,0:T(8,128)S(1)}, f32[1,16,64]{2,1,0:T(8,128)S(1)}, u32[]{:S(2)}, u32[]{:S(2)}) collective-permute-start(f32[1,16,64]{2,1,0:T(8,128)S(1)} %get-tuple-element.18), channel_id=1, source_target_pairs={{1,0},{2,1},{3,2},{4,3},{5,4},{6,5},{7,6},{9,8},{10,9},{11,10},{12... | collective-permute-start | bytes 12296 | tf_op jit(solution)/shard_map/ppermute | solution.py:21
  159.4 4.5 %collective-permute-start.14 = (f32[2,16,64]{2,1,0:T(8,128)S(1)}, f32[2,16,64]{2,1,0:T(8,128)S(1)}, u32[]{:S(2)}, u32[]{:S(2)}) collective-permute-start(f32[2,16,64]{2,1,0:T(8,128)S(1)} %fusion.70), channel_id=1, source_target_pairs={{0,8},{8,16},{16,24},{1,9},{9,17},{17,25},{2,10},{10,18},{18,26},{... | collective-permute-start | bytes 24584 | tf_op jit(solution)/shard_map/ppermute | solution.py:29
  164.0 5.0 %collective-permute-start.16 = (f32[1,16,64]{2,1,0:T(8,128)S(1)}, f32[1,16,64]{2,1,0:T(8,128)S(1)}, u32[]{:S(2)}, u32[]{:S(2)}) collective-permute-start(f32[1,16,64]{2,1,0:T(8,128)S(1)} %get-tuple-element.15), channel_id=1, source_target_pairs={{0,1},{1,2},{2,3},{3,4},{4,5},{5,6},{6,7},{8,9},{9,10},{10,11},{11... | collective-permute-start | bytes 12296 | tf_op jit(solution)/shard_map/ppermute | solution.py:18
  167.1 5.9 %collective-permute-start.15 = (f32[1,16,64]{2,1,0:T(8,128)S(1)}, f32[1,16,64]{2,1,0:T(8,128)S(1)}, u32[]{:S(2)}, u32[]{:S(2)}) collective-permute-start(f32[1,16,64]{2,1,0:T(8,128)S(1)} %get-tuple-element.16), channel_id=1, source_target_pairs={{1,0},{2,1},{3,2},{4,3},{5,4},{6,5},{7,6},{9,8},{10,9},{11,10},{12... | collective-permute-start | bytes 12296 | tf_op jit(solution)/shard_map/ppermute | solution.py:21
where the time goes:
time: 175 us
  local copies, waits for them, and re-layouts  61.7 us (35%)
  starting transfers between devices  43.1 us (25%)
  other arithmetic  39.7 us (23%)
  waiting for transfers between devices  29.6 us (17%)
    reshape x2, local copies, waits for them, and re-layouts, restrict(): field.reshape(planes // coarsen, coarsen, rows // coarsen, coarsen, cols...  37.3 us
    ppermute x7, starting transfers between devices, with_halo(): lax.ppermute(lax.slice_in_dim(block, block.shape[dim] - width, None, axis...  25.7 us
    reduce_sum x3, other arithmetic, restrict(): return jnp.mean(blocks, axis=(1, 3, 5))  21.2 us
    another operation x1, local copies, waits for them, and re-layouts, restrict(): field.reshape(planes // coarsen, coarsen, rows // coarsen, coarsen, cols...  18.6 us
    ppermute x7, waiting for transfers between devices, with_halo(): lax.ppermute(lax.slice_in_dim(block, 0, width, axis=dim), axis, backward)  13.7 us
    ppermute x7, starting transfers between devices, with_halo(): lax.ppermute(lax.slice_in_dim(block, 0, width, axis=dim), axis, backward)  13.6 us
    ppermute x3, waiting for transfers between devices, passed_along(): return lax.ppermute(block, axis, route)  9.54 us
    mul x16, other arithmetic, plane_div(): flux = 0.5 * (upper_c + lower_c) * (upper - lower)  6.34 us
  transfers between devices with their start and end apart: 17, of which 8 were waited for; matrix products, arithmetic and copies ran while one was open for 31% of the time, Pallas kernels for 0%

commit v1 on v0

v1 whole, which is shorter than its diff:
```python
import functools
import jax
import jax.numpy as jnp
from jax import lax
from jax.experimental import pallas as pl
from jax.experimental.pallas import tpu as pltpu
from jax.sharding import PartitionSpec as P

FSTEPS = 4
fine_rate = 0.1
coarsen = 4
LANES = 128
MESH = pl.DeviceIdType.MESH
HIGHEST = lax.Precision.HIGHEST


def group_matrix(shape, dim):
    fine = lax.broadcasted_iota(jnp.int32, shape, 1 - dim)
    coarse = lax.broadcasted_iota(jnp.int32, shape, dim)
    first = fine - coarse * coarsen
    return jnp.where((first >= 0) & (first < coarsen), 1.0, 0.0).astype(jnp.float32)


def dot(a, b):
    return jnp.dot(a, b, precision=HIGHEST, preferred_element_type=jnp.float32)


def kernel(
    slices, slabs, reach,
    states, conduct, out,
    field, cond, ax, ay, az,
    block, ext, first, jump, jumps,
    load_sem, fsend, frecv, csend, crecv, esend, erecv, ssend, srecv, jsend, jrecv,
):
    tm = lax.axis_index("tm")
    me = lax.axis_index("space")
    _, planes, rows, cols = states.shape
    crows, ccols = rows // coarsen, cols // coarsen
    cplanes = planes // coarsen
    pack = LANES // ccols
    far = reach(slices)
    blocks = 2 * far + 1
    offsets = [d for d in range(-far, far + 1) if d != 0]

    has_low = me > 0
    has_high = me < slabs - 1

    def inside(d):
        return (me + d >= 0) & (me + d < slabs)

    def later(delta):
        return tm + delta < slices

    load_v = pltpu.make_async_copy(states.at[0], field.at[0, pl.ds(1, planes)], load_sem.at[0])
    load_c = pltpu.make_async_copy(conduct, cond.at[pl.ds(1, planes)], load_sem.at[1])
    load_v.start()
    load_c.start()

    zero_plane = jnp.zeros((rows, cols), jnp.float32)

    @pl.when(jnp.logical_not(has_low))
    def _():
        cond[0] = zero_plane
        for k in range(FSTEPS):
            field[k, 0] = zero_plane

    @pl.when(jnp.logical_not(has_high))
    def _():
        cond[planes + 1] = zero_plane
        for k in range(FSTEPS):
            field[k, planes + 1] = zero_plane

    ext[...] = jnp.zeros(ext.shape, jnp.float32)
    jumps[...] = jnp.zeros(jumps.shape, jnp.float32)

    barrier = pltpu.get_barrier_semaphore()
    peers = [(0, d) for d in offsets]
    for delta in range(1, slices):
        for d in range(-reach(delta), reach(delta) + 1):
            peers += [(delta, d), (-delta, d)]
    count = jnp.int32(0)
    for dt, d in peers:
        there = inside(d) & (tm + dt >= 0) & (tm + dt < slices)

        @pl.when(there)
        def _(dt=dt, d=d):
            pl.semaphore_signal(barrier, inc=1, device_id=(tm + dt, me + d), device_id_type=MESH)

        count = count + there.astype(jnp.int32)
    pl.semaphore_wait(barrier, count)

    def halo(k, side):
        step = 1 if side == 0 else -1
        if k == 0:
            src = states.at[0, planes - 1 if side == 0 else 0]
        else:
            src = field.at[k, planes if side == 0 else 1]
        return pltpu.make_async_remote_copy(
            src_ref=src, dst_ref=field.at[k, 0 if side == 0 else planes + 1],
            send_sem=fsend.at[k, side], recv_sem=frecv.at[k, side],
            device_id=(tm, me + step), device_id_type=MESH,
        )

    def halo_c(side):
        step = 1 if side == 0 else -1
        return pltpu.make_async_remote_copy(
            src_ref=conduct.at[planes - 1 if side == 0 else 0],
            dst_ref=cond.at[0 if side == 0 else planes + 1],
            send_sem=csend.at[side], recv_sem=crecv.at[side],
            device_id=(tm, me + step), device_id_type=MESH,
        )

    sends_side = (has_high, has_low)
    hears_side = (has_low, has_high)

    for side in range(2):
        @pl.when(sends_side[side])
        def _(side=side):
            halo_c(side).start()
            halo(0, side).start()

    lane = lax.broadcasted_iota(jnp.int32, (crows, LANES), 1)
    gather_y = group_matrix((cols, LANES), 1)
    gather_x = group_matrix((cplanes * crows, cplanes * rows), 0)

    def restrict(ref, lead):
        sums = []
        for c in range(cplanes):
            total = ref[(*lead, 1 + c * coarsen)]
            for j in range(1, coarsen):
                total = total + ref[(*lead, 1 + c * coarsen + j)]
            sums.append(total)
        lanes = dot(jnp.concatenate(sums, axis=0), gather_y)
        return dot(gather_x, lanes) * (1.0 / coarsen**3)

    def packed(value):
        parts = []
        for g in range(cplanes // pack):
            total = None
            for j in range(pack):
                c = g * pack + j
                piece = value[c * crows : (c + 1) * crows]
                if j:
                    piece = pltpu.roll(piece, j * ccols, 1)
                total = piece if total is None else total + piece
            parts.append(total)
        return jnp.concatenate(parts, axis=0) if len(parts) > 1 else parts[0]

    def unpacked(values):
        parts = []
        for value in values:
            for g in range(cplanes // pack):
                piece = value[g * crows : (g + 1) * crows]
                for j in range(pack):
                    moved = pltpu.roll(piece, LANES - j * ccols, 1) if j else piece
                    parts.append(jnp.where(lane < ccols, moved, 0.0))
        return jnp.concatenate(parts, axis=0)

    def early(d):
        return pltpu.make_async_remote_copy(
            src_ref=block, dst_ref=ext.at[far - d],
            send_sem=esend.at[far + d], recv_sem=erecv.at[far - d],
            device_id=(tm, me + d), device_id_type=MESH,
        )

    load_v.wait()
    load_c.wait()
    block[0] = packed(restrict(field, (0,)))
    block[1] = packed(restrict(cond, ()))
    for d in offsets:
        @pl.when(inside(d))
        def _(d=d):
            early(d).start()
    ext[far] = block[...]

    half = 0.5 * fine_rate
    row_face = lax.broadcasted_iota(jnp.int32, (rows, cols), 0) < rows - 1
    col_face = lax.broadcasted_iota(jnp.int32, (rows, cols), 1) < cols - 1

    def faces(p, carry):
        c = cond[p]
        ax[p - 1] = jnp.where(row_face, half * (c + pltpu.roll(c, rows - 1, 0)), 0.0)
        ay[p - 1] = jnp.where(col_face, half * (c + pltpu.roll(c, cols - 1, 1)), 0.0)
        return carry

    def faces_z(p, carry):
        az[p] = half * (cond[p] + cond[p + 1])
        return carry

    lax.fori_loop(1, planes + 1, faces, 0)
    lax.fori_loop(1, planes, faces_z, 0)

    def advance(k, p):
        v = field[k, p]
        fx = ax[p - 1] * (pltpu.roll(v, rows - 1, 0) - v)
        fy = ay[p - 1] * (pltpu.roll(v, cols - 1, 1) - v)
        high = az[p] * (field[k, p + 1] - v)
        low = az[p - 1] * (v - field[k, p - 1])
        div = (high - low) + (fx - pltpu.roll(fx, 1, 0)) + (fy - pltpu.roll(fy, 1, 1))
        field[k + 1, p] = v + div

    def fine_step(k):
        for side in range(2):
            edge = 1 if side == 0 else planes

            @pl.when(hears_side[side])
            def _(side=side):
                if k == 0:
                    halo_c(side).wait_recv()
                halo(k, side).wait_recv()

            if k == 0:
                low_plane = 0 if side == 0 else planes
                scale = jnp.where(hears_side[side], half, 0.0)
                az[low_plane] = scale * (cond[low_plane] + cond[low_plane + 1])
            advance(k, edge)
            if k < FSTEPS - 1:
                @pl.when(sends_side[1 - side])
                def _(side=side):
                    halo(k + 1, 1 - side).start()

        def inner(p, carry):
            advance(k, p)
            return carry

        lax.fori_loop(2, planes, inner, 0)

    total_rows = blocks * cplanes * crows

    def coarse_faces():
        c = unpacked([ext[b, 1] for b in range(blocks)])
        half_c = 0.5 * fine_rate * FSTEPS / 16.0
        row = lax.broadcasted_iota(jnp.int32, (total_rows, LANES), 0)
        col = lax.broadcasted_iota(jnp.int32, (total_rows, LANES), 1)
        cx = jnp.where(row % crows < crows - 1, half_c * (c + pltpu.roll(c, total_rows - 1, 0)), 0.0)
        cy = jnp.where(col < ccols - 1, half_c * (c + pltpu.roll(c, LANES - 1, 1)), 0.0)
        ahead = row + (me - far) * (cplanes * crows)
        valid = (ahead >= 0) & (ahead < (slabs * cplanes - 1) * crows) & (row < total_rows - crows)
        cz = jnp.where(valid, half_c * (c + pltpu.roll(c, total_rows - crows, 0)), 0.0)
        return cx, cy, cz

    def propagate(w, coef):
        cx, cy, cz = coef
        fx = cx * (pltpu.roll(w, total_rows - 1, 0) - w)
        fy = cy * (pltpu.roll(w, LANES - 1, 1) - w)
        fz = cz * (pltpu.roll(w, total_rows - crows, 0) - w)
        div = (fz - pltpu.roll(fz, crows, 0)) + (fx - pltpu.roll(fx, 1, 0)) + (fy - pltpu.roll(fy, 1, 1))
        return w + div

    centre = slice(far * cplanes * crows, (far + 1) * cplanes * crows)

    def start_copy(delta):
        return pltpu.make_async_remote_copy(
            src_ref=first.at[0], dst_ref=first.at[1],
            send_sem=ssend.at[delta - 1], recv_sem=srecv,
            device_id=(tm + delta, me), device_id_type=MESH,
        )

    fine_step(0)

    for d in offsets:
        @pl.when(inside(d))
        def _(d=d):
            early(-d).wait_recv()
    for b in range(blocks):
        first[0, b] = ext[b, 0]
    for delta in range(1, slices):
        @pl.when((tm == 0) & (delta < slices))
        def _(delta=delta):
            start_copy(delta).start()

    fine_step(1)
    coef = coarse_faces()
    coarse_old = propagate(unpacked([first[0, b] for b in range(blocks)]), coef)[centre]
    fine_step(2)
    fine_step(3)

    jump[...] = packed(restrict(field, (FSTEPS,)) - coarse_old)

    def jump_copy(delta, d):
        at = (delta - 1) * blocks
        return pltpu.make_async_remote_copy(
            src_ref=jump, dst_ref=jumps.at[delta - 1, far - d],
            send_sem=jsend.at[at + far + d], recv_sem=jrecv.at[at + far - d],
            device_id=(tm + delta, me + d), device_id_type=MESH,
        )

    routes = [
        (delta, d)
        for delta in range(1, slices)
        for d in sorted(range(-reach(delta), reach(delta) + 1), key=lambda d: -abs(d))
    ]
    for delta, d in routes:
        @pl.when(later(delta) & inside(d))
        def _(delta=delta, d=d):
            jump_copy(delta, d).start()

    @pl.when(tm > 0)
    def _():
        start_copy(1).wait_recv()

    @pl.when(tm == 0)
    def _():
        first[1] = first[0]

    w = unpacked([first[1, b] for b in range(blocks)])
    for delta in range(slices - 1, 0, -1):
        for at, d in routes:
            if at == delta:
                @pl.when((tm >= delta) & inside(d))
                def _(delta=delta, d=d):
                    jump_copy(delta, -d).wait_recv()
        new = propagate(w, coef) + unpacked([jumps[delta - 1, b] for b in range(blocks)])
        w = jnp.where(tm >= delta, new, w)
    change = propagate(w, coef)[centre] - coarse_old

    spread_x = group_matrix((cplanes * rows, cplanes * crows), 1)
    spread_y = group_matrix((LANES, cols), 0)
    spread = dot(dot(spread_x, change), spread_y)
    stores = []
    for c in range(cplanes):
        piece = spread[c * rows : (c + 1) * rows]
        at = 1 + c * coarsen
        for j in range(coarsen):
            field[FSTEPS, at + j] = field[FSTEPS, at + j] + piece
        store = pltpu.make_async_copy(
            field.at[FSTEPS, pl.ds(at, coarsen)],
            out.at[0, pl.ds(c * coarsen, coarsen)],
            load_sem.at[2 + c],
        )
        store.start()
        stores.append(store)

    for side in range(2):
        @pl.when(sends_side[side])
        def _(side=side):
            halo_c(side).wait_send()
            for k in range(FSTEPS):
                halo(k, side).wait_send()
    for d in offsets:
        @pl.when(inside(d))
        def _(d=d):
            early(d).wait_send()
    for delta in range(1, slices):
        @pl.when(tm == 0)
        def _(delta=delta):
            start_copy(delta).wait_send()
    for delta, d in routes:
        @pl.when(later(delta) & inside(d))
        def _(delta=delta, d=d):
            jump_copy(delta, d).wait_send()
    for store in stores:
        store.wait()


def per_device(slices, slabs, states, conductivity):
    _, planes, rows, cols = states.shape
    cplanes, crows = planes // coarsen, rows // coarsen
    pack = LANES // (cols // coarsen)
    packed_rows = cplanes // pack * crows

    def reach(delta):
        return -(-delta // cplanes)

    far = reach(slices)
    blocks = 2 * far + 1
    f32 = jnp.float32
    dma = pltpu.SemaphoreType.DMA
    hops = max(slices - 1, 1)
    return pl.pallas_call(
        functools.partial(kernel, slices, slabs, reach),
        out_shape=jax.ShapeDtypeStruct(states.shape, f32),
        in_specs=[pl.BlockSpec(memory_space=pl.ANY)] * 2,
        out_specs=pl.BlockSpec(memory_space=pl.ANY),
        scratch_shapes=[
            pltpu.VMEM((FSTEPS + 1, planes + 2, rows, cols), f32),
            pltpu.VMEM((planes + 2, rows, cols), f32),
            pltpu.VMEM((planes, rows, cols), f32),
            pltpu.VMEM((planes, rows, cols), f32),
            pltpu.VMEM((planes + 1, rows, cols), f32),
            pltpu.VMEM((2, packed_rows, LANES), f32),
            pltpu.VMEM((blocks, 2, packed_rows, LANES), f32),
            pltpu.VMEM((2, blocks, packed_rows, LANES), f32),
            pltpu.VMEM((packed_rows, LANES), f32),
            pltpu.VMEM((hops, blocks, packed_rows, LANES), f32),
            dma((2 + cplanes,)),
            dma((FSTEPS, 2)),
            dma((FSTEPS, 2)),
            dma((2,)),
            dma((2,)),
            dma((blocks,)),
            dma((blocks,)),
            dma((hops,)),
            dma,
            dma((hops * blocks,)),
            dma((hops * blocks,)),
        ],
        compiler_params=pltpu.CompilerParams(
            collective_id=0, has_side_effects=True, vmem_limit_bytes=32 * 1024 * 1024
        ),
    )(states, conductivity)


def solution(mesh):
    in_specs = (P("tm", "space", None, None), P("space", None, None))
    out_specs = P("tm", "space", None, None)
    return jax.shard_map(
        functools.partial(per_device, mesh.shape["tm"], mesh.shape["space"]),
        mesh=mesh, in_specs=in_specs, out_specs=out_specs, check_vma=False,
    )
```

time: 175 us -> 30.8 us (0.18)
  local copies, waits for them, and re-layouts: 61.7 us -> 2.88 us
  starting transfers between devices: 43.1 us -> 0 us
  other arithmetic: 39.7 us -> 0 us
  waiting for transfers between devices: 29.6 us -> 0 us
  Pallas kernels: 0 us -> 27.7 us
    ppermute x17 -> x0, starting transfers between devices: 43.1 us -> none  [the longest x7 25.7 us: with_halo(): lax.ppermute(lax.slice_in_dim(block, block.shape[dim] - width, None, axis...]
    reshape x3 -> x0, local copies, waits for them, and re-layouts: 37.4 us -> none  [the longest x2 37.3 us: restrict(): field.reshape(planes // coarsen, coarsen, rows // coarsen, coarsen, cols...]
    ppermute x17 -> x0, waiting for transfers between devices: 29.6 us -> none  [the longest x7 13.7 us: with_halo(): lax.ppermute(lax.slice_in_dim(block, 0, width, axis=dim), axis, backward)]
    pallas_call x0 -> x1, Pallas kernels: none -> 27.7 us  [per_device(): pl.pallas_call(functools.partial(kernel, slices, slabs, reach), out_shape...]
    reduce_sum x3 -> x0, other arithmetic: 21.2 us -> none  [restrict(): return jnp.mean(blocks, axis=(1, 3, 5))]
    another operation x1 -> x0, local copies, waits for them, and re-layouts: 18.6 us -> none  [restrict(): field.reshape(planes // coarsen, coarsen, rows // coarsen, coarsen, cols...]
    mul x29 -> x0, other arithmetic: 11.1 us -> none  [the longest x16 6.34 us: plane_div(): flux = 0.5 * (upper_c + lower_c) * (upper - lower)]
    add x8 -> x0, other arithmetic: 5.29 us -> none  [the longest x4 4.96 us: padded_step(): return centre + step_rate * (div_z + div_x + div_y)]
  transfers between devices with their start and end apart: 17 -> 0, of which waited for: 8 -> 0; matrix products, arithmetic and copies ran while one was open for 31% -> 0% of each run, Pallas kernels for 0% -> 0%
where the time goes in v1:
time: 30.8 us; the launch traced here: 30.6 us
  Pallas kernels  27.7 us (90%)
  local copies, waits for them, and re-layouts  2.88 us (9%)
    pallas_call x1, Pallas kernels, per_device(): pl.pallas_call(functools.partial(kernel, slices, slabs, reach), out_shape...  27.7 us
    unnamed x5, local copies, waits for them, and re-layouts  2.88 us

profile of v1, /device:TPU:27, one launch (start us, length us, event | category | flops | bytes accessed | tf_op | source)
XLA Modules:
  0.0 30.6 jit_solution(3242376682839869868)
XLA Ops:
  0.0 0.0 copy-start
  0.0 1.0 %copy-done = f32[1,8,64,256]{3,2,1,0:T(8,128)S(1)} copy-done((f32[1,8,64,256]{3,2,1,0:T(8,128)S(1)}, f32[1,8,64,256]{3,2,1,0:T(8,128)}, u32[]{:S(2)}) %copy-start) | copy-done | bytes 524312
  1.0 0.0 copy-start.1
  1.0 1.0 %copy-done.1 = f32[8,64,256]{2,1,0:T(8,128)S(1)} copy-done((f32[8,64,256]{2,1,0:T(8,128)S(1)}, f32[8,64,256]{2,1,0:T(8,128)}, u32[]{:S(2)}) %copy-start.1) | copy-done | bytes 524312
  2.1 27.7 %shard_map.28 = f32[1,8,64,256]{3,2,1,0:T(8,128)S(1)} custom-call(f32[1,8,64,256]{3,2,1,0:T(8,128)S(1)} %copy-done, f32[8,64,256]{2,1,0:T(8,128)S(1)} %copy-done.1), custom_call_target="tpu_custom_call" | custom-call | tf_op jit(solution)/shard_map/pallas_call | solution.py:370
  29.8 0.8 %copy.4 = f32[1,8,64,256]{3,2,1,0:T(8,128)} copy(f32[1,8,64,256]{3,2,1,0:T(8,128)S(1)} %shard_map.28) | data formatting | bytes 1048576
Async XLA Ops:
  0.0 1.0 %copy-start = (f32[1,8,64,256]{3,2,1,0:T(8,128)S(1)}, f32[1,8,64,256]{3,2,1,0:T(8,128)}, u32[]{:S(2)}) copy-start(f32[1,8,64,256]{3,2,1,0:T(8,128)} %states.1) | copy-start | bytes 1572868
  1.0 1.0 %copy-start.1 = (f32[8,64,256]{2,1,0:T(8,128)S(1)}, f32[8,64,256]{2,1,0:T(8,128)}, u32[]{:S(2)}) copy-start(f32[8,64,256]{2,1,0:T(8,128)} %conduct.1) | copy-start | bytes 1572868

commit v2 on v1

--- a/solution.py
+++ b/solution.py
@@ -30,7 +30,7 @@
     states, conduct, out,
     field, cond, ax, ay, az,
     block, ext, first, jump, jumps,
-    load_sem, fsend, frecv, csend, crecv, esend, erecv, ssend, srecv, jsend, jrecv,
+    load_sem, fsend, frecv, csend, crecv, esend, erecv, ssend, srecv, jsend, jrecv, token,
 ):
     tm = lax.axis_index("tm")
     me = lax.axis_index("space")
@@ -74,10 +74,8 @@
     jumps[...] = jnp.zeros(jumps.shape, jnp.float32)
 
     barrier = pltpu.get_barrier_semaphore()
-    peers = [(0, d) for d in offsets]
-    for delta in range(1, slices):
-        for d in range(-reach(delta), reach(delta) + 1):
-            peers += [(delta, d), (-delta, d)]
+    near = max(1, far - 1)
+    peers = [(0, d) for d in range(-near, near + 1) if d != 0] + [(1, 0), (-1, 0)]
     count = jnp.int32(0)
     for dt, d in peers:
         there = inside(d) & (tm + dt >= 0) & (tm + dt < slices)
@@ -167,11 +165,15 @@
     load_c.wait()
     block[0] = packed(restrict(field, (0,)))
     block[1] = packed(restrict(cond, ()))
-    for d in offsets:
-        @pl.when(inside(d))
-        def _(d=d):
-            early(d).start()
     ext[far] = block[...]
+
+    def early_send(distances):
+        for d in distances:
+            @pl.when(inside(d))
+            def _(d=d):
+                early(d).start()
+
+    early_send([d for d in offsets if abs(d) <= near])
 
     half = 0.5 * fine_rate
     row_face = lax.broadcasted_iota(jnp.int32, (rows, cols), 0) < rows - 1
@@ -256,24 +258,53 @@
             device_id=(tm + delta, me), device_id_type=MESH,
         )
 
+    def pass_token(r):
+        @pl.when((tm > 0) & (tm + r < slices))
+        def _():
+            pl.semaphore_signal(token.at[r], inc=1, device_id=(tm - 1, me), device_id_type=MESH)
+
+    def take_token(r):
+        @pl.when(tm + 1 + r < slices)
+        def _():
+            pl.semaphore_wait(token.at[r], 1)
+
+    def send_start(delta):
+        @pl.when(tm == 0)
+        def _():
+            start_copy(delta).start()
+
     fine_step(0)
-
+    early_send([d for d in offsets if abs(d) > near])
+    if slices > 1:
+        pass_token(0)
+
+    fine_step(1)
     for d in offsets:
         @pl.when(inside(d))
         def _(d=d):
             early(-d).wait_recv()
     for b in range(blocks):
         first[0, b] = ext[b, 0]
-    for delta in range(1, slices):
-        @pl.when((tm == 0) & (delta < slices))
-        def _(delta=delta):
-            start_copy(delta).start()
-
-    fine_step(1)
+    for r in range(slices - 2):
+        if r == 0:
+            take_token(0)
+            pass_token(1)
+    if slices > 1:
+        if slices == 2:
+            take_token(0)
+        send_start(1)
     coef = coarse_faces()
     coarse_old = propagate(unpacked([first[0, b] for b in range(blocks)]), coef)[centre]
     fine_step(2)
+    for r in range(1, slices - 1):
+        take_token(r)
+        if r + 1 < slices - 1:
+            pass_token(r + 1)
+        if r < slices - 2:
+            send_start(r + 1)
     fine_step(3)
+    if slices > 2:
+        send_start(slices - 1)
 
     jump[...] = packed(restrict(field, (FSTEPS,)) - coarse_old)
 
@@ -370,7 +401,7 @@
     return pl.pallas_call(
         functools.partial(kernel, slices, slabs, reach),
         out_shape=jax.ShapeDtypeStruct(states.shape, f32),
-        in_specs=[pl.BlockSpec(memory_space=pl.ANY)] * 2,
+        in_specs=[pl.BlockSpec(memory_space=pltpu.HBM)] * 2,
         out_specs=pl.BlockSpec(memory_space=pl.ANY),
         scratch_shapes=[
             pltpu.VMEM((FSTEPS + 1, planes + 2, rows, cols), f32),
@@ -394,6 +425,7 @@
             dma,
             dma((hops * blocks,)),
             dma((hops * blocks,)),
+            pltpu.SemaphoreType.REGULAR((hops,)),
         ],
         compiler_params=pltpu.CompilerParams(
             collective_id=0, has_side_effects=True, vmem_limit_bytes=32 * 1024 * 1024

time: 30.8 us -> 27.6 us (0.90)
  Pallas kernels: 27.7 us -> 24.4 us
    pallas_call x1, Pallas kernels: 27.7 us -> 24.4 us  [per_device(): pl.pallas_call(functools.partial(kernel, slices, slabs, reach), out_shape...]
where the time goes in v2:
time: 27.6 us; the launch traced here: 27.2 us
  Pallas kernels  24.4 us (88%)
  local copies, waits for them, and re-layouts  2.88 us (10%)
    pallas_call x1, Pallas kernels, per_device(): pl.pallas_call(functools.partial(kernel, slices, slabs, reach), out_shape...  24.4 us
    unnamed x5, local copies, waits for them, and re-layouts  2.88 us

profile of v2, /device:TPU:27, one launch (start us, length us, event | category | flops | bytes accessed | tf_op | source)
XLA Modules:
  0.0 27.2 jit_solution(540369823185029227)
XLA Ops:
  0.0 0.0 copy-start
  0.0 1.0 %copy-done = f32[1,8,64,256]{3,2,1,0:T(8,128)S(1)} copy-done((f32[1,8,64,256]{3,2,1,0:T(8,128)S(1)}, f32[1,8,64,256]{3,2,1,0:T(8,128)}, u32[]{:S(2)}) %copy-start) | copy-done | bytes 524312
  1.0 0.0 copy-start.1
  1.0 1.0 %copy-done.1 = f32[8,64,256]{2,1,0:T(8,128)S(1)} copy-done((f32[8,64,256]{2,1,0:T(8,128)S(1)}, f32[8,64,256]{2,1,0:T(8,128)}, u32[]{:S(2)}) %copy-start.1) | copy-done | bytes 524312
  2.1 24.4 %shard_map.28 = f32[1,8,64,256]{3,2,1,0:T(8,128)S(1)} custom-call(f32[1,8,64,256]{3,2,1,0:T(8,128)S(1)} %copy-done, f32[8,64,256]{2,1,0:T(8,128)S(1)} %copy-done.1), custom_call_target="tpu_custom_call" | custom-call | tf_op jit(solution)/shard_map/pallas_call | solution.py:401
  26.4 0.8 %copy.4 = f32[1,8,64,256]{3,2,1,0:T(8,128)} copy(f32[1,8,64,256]{3,2,1,0:T(8,128)S(1)} %shard_map.28) | data formatting | bytes 1048576
Async XLA Ops:
  0.0 1.0 %copy-start = (f32[1,8,64,256]{3,2,1,0:T(8,128)S(1)}, f32[1,8,64,256]{3,2,1,0:T(8,128)}, u32[]{:S(2)}) copy-start(f32[1,8,64,256]{3,2,1,0:T(8,128)} %states.1) | copy-start | bytes 1572868
  1.0 1.0 %copy-start.1 = (f32[8,64,256]{2,1,0:T(8,128)S(1)}, f32[8,64,256]{2,1,0:T(8,128)}, u32[]{:S(2)}) copy-start(f32[8,64,256]{2,1,0:T(8,128)} %conduct.1) | copy-start | bytes 1572868

commit v3 on v2

--- a/solution.py
+++ b/solution.py
@@ -10,6 +10,8 @@
 fine_rate = 0.1
 coarsen = 4
 LANES = 128
+PARTS = 2
+EDGE = 8
 MESH = pl.DeviceIdType.MESH
 HIGHEST = lax.Precision.HIGHEST
 
@@ -87,15 +89,18 @@
         count = count + there.astype(jnp.int32)
     pl.semaphore_wait(barrier, count)
 
-    def halo(k, side):
+    part = rows // PARTS
+
+    def halo(k, side, q):
         step = 1 if side == 0 else -1
+        at = pl.ds(q * part, part)
         if k == 0:
-            src = states.at[0, planes - 1 if side == 0 else 0]
+            src = states.at[0, planes - 1 if side == 0 else 0, at]
         else:
-            src = field.at[k, planes if side == 0 else 1]
+            src = field.at[k, planes if side == 0 else 1, at]
         return pltpu.make_async_remote_copy(
-            src_ref=src, dst_ref=field.at[k, 0 if side == 0 else planes + 1],
-            send_sem=fsend.at[k, side], recv_sem=frecv.at[k, side],
+            src_ref=src, dst_ref=field.at[k, 0 if side == 0 else planes + 1, at],
+            send_sem=fsend.at[k, side, q], recv_sem=frecv.at[k, side, q],
             device_id=(tm, me + step), device_id_type=MESH,
         )
 
@@ -115,7 +120,8 @@
         @pl.when(sends_side[side])
         def _(side=side):
             halo_c(side).start()
-            halo(0, side).start()
+            for q in range(PARTS):
+                halo(0, side, q).start()
 
     lane = lax.broadcasted_iota(jnp.int32, (crows, LANES), 1)
     gather_y = group_matrix((cols, LANES), 1)
@@ -201,31 +207,54 @@
         div = (high - low) + (fx - pltpu.roll(fx, 1, 0)) + (fy - pltpu.roll(fy, 1, 1))
         field[k + 1, p] = v + div
 
-    def fine_step(k):
-        for side in range(2):
-            edge = 1 if side == 0 else planes
-
-            @pl.when(hears_side[side])
-            def _(side=side):
-                if k == 0:
-                    halo_c(side).wait_recv()
-                halo(k, side).wait_recv()
-
-            if k == 0:
-                low_plane = 0 if side == 0 else planes
-                scale = jnp.where(hears_side[side], half, 0.0)
-                az[low_plane] = scale * (cond[low_plane] + cond[low_plane + 1])
-            advance(k, edge)
-            if k < FSTEPS - 1:
-                @pl.when(sends_side[1 - side])
-                def _(side=side):
-                    halo(k + 1, 1 - side).start()
-
+    def advance_part(k, p, q):
+        start, stop = q * part, (q + 1) * part
+        low_row, high_row = max(start - EDGE, 0), min(stop + EDGE, rows)
+        size = high_row - low_row
+        mine = slice(start - low_row, stop - low_row)
+        window = field[k, p, low_row:high_row]
+        inner_face = lax.broadcasted_iota(jnp.int32, (size, cols), 0) < size - 1
+        fx = jnp.where(inner_face, ax[p - 1, low_row:high_row] * (pltpu.roll(window, size - 1, 0) - window), 0.0)
+        div_x = (fx - pltpu.roll(fx, 1, 0))[mine]
+        v = window[mine]
+        fy = ay[p - 1, start:stop] * (pltpu.roll(v, cols - 1, 1) - v)
+        high = az[p, start:stop] * (field[k, p + 1, start:stop] - v)
+        low = az[p - 1, start:stop] * (v - field[k, p - 1, start:stop])
+        div = (high - low) + div_x + (fy - pltpu.roll(fy, 1, 1))
+        field[k + 1, p, start:stop] = v + div
+
+    def inner_planes(k):
         def inner(p, carry):
             advance(k, p)
             return carry
 
         lax.fori_loop(2, planes, inner, 0)
+
+    def fine_step(k):
+        if k == FSTEPS - 1:
+            inner_planes(k)
+        for q in range(PARTS):
+            for side in range(2):
+                edge = 1 if side == 0 else planes
+
+                @pl.when(hears_side[side])
+                def _(side=side):
+                    if k == 0 and q == 0:
+                        halo_c(side).wait_recv()
+                    halo(k, side, q).wait_recv()
+
+                if k == 0 and q == 0:
+                    low_plane = 0 if side == 0 else planes
+                    scale = jnp.where(hears_side[side], half, 0.0)
+                    az[low_plane] = scale * (cond[low_plane] + cond[low_plane + 1])
+                advance_part(k, edge, q)
+                if k < FSTEPS - 1:
+                    @pl.when(sends_side[1 - side])
+                    def _(side=side):
+                        halo(k + 1, 1 - side, q).start()
+
+        if k < FSTEPS - 1:
+            inner_planes(k)
 
     total_rows = blocks * cplanes * crows
 
@@ -367,7 +396,8 @@
         def _(side=side):
             halo_c(side).wait_send()
             for k in range(FSTEPS):
-                halo(k, side).wait_send()
+                for q in range(PARTS):
+                    halo(k, side, q).wait_send()
     for d in offsets:
         @pl.when(inside(d))
         def _(d=d):
@@ -415,8 +445,8 @@
             pltpu.VMEM((packed_rows, LANES), f32),
             pltpu.VMEM((hops, blocks, packed_rows, LANES), f32),
             dma((2 + cplanes,)),
-            dma((FSTEPS, 2)),
-            dma((FSTEPS, 2)),
+            dma((FSTEPS, 2, PARTS)),
+            dma((FSTEPS, 2, PARTS)),
             dma((2,)),
             dma((2,)),
             dma((blocks,)),

time: 27.6 us -> 26.7 us (0.967)
  Pallas kernels: 24.4 us -> 23.7 us
    pallas_call x1, Pallas kernels: 24.4 us -> 23.7 us  [per_device(): pl.pallas_call(functools.partial(kernel, slices, slabs, reach), out_shape...]
where the time goes in v3:
time: 26.7 us; the launch traced here: 26.5 us
  Pallas kernels  23.7 us (89%)
  local copies, waits for them, and re-layouts  2.88 us (11%)
    pallas_call x1, Pallas kernels, per_device(): pl.pallas_call(functools.partial(kernel, slices, slabs, reach), out_shape...  23.7 us
    unnamed x5, local copies, waits for them, and re-layouts  2.88 us

profile of v3, /device:TPU:27, one launch (start us, length us, event | category | flops | bytes accessed | tf_op | source)
XLA Modules:
  0.0 26.5 jit_solution(6128406205670253743)
XLA Ops:
  0.0 0.0 copy-start
  0.0 1.0 %copy-done = f32[1,8,64,256]{3,2,1,0:T(8,128)S(1)} copy-done((f32[1,8,64,256]{3,2,1,0:T(8,128)S(1)}, f32[1,8,64,256]{3,2,1,0:T(8,128)}, u32[]{:S(2)}) %copy-start) | copy-done | bytes 524312
  1.0 0.0 copy-start.1
  1.0 1.0 %copy-done.1 = f32[8,64,256]{2,1,0:T(8,128)S(1)} copy-done((f32[8,64,256]{2,1,0:T(8,128)S(1)}, f32[8,64,256]{2,1,0:T(8,128)}, u32[]{:S(2)}) %copy-start.1) | copy-done | bytes 524312
  2.1 23.7 %shard_map.28 = f32[1,8,64,256]{3,2,1,0:T(8,128)S(1)} custom-call(f32[1,8,64,256]{3,2,1,0:T(8,128)S(1)} %copy-done, f32[8,64,256]{2,1,0:T(8,128)S(1)} %copy-done.1), custom_call_target="tpu_custom_call" | custom-call | tf_op jit(solution)/shard_map/pallas_call | solution.py:431
  25.7 0.8 %copy.4 = f32[1,8,64,256]{3,2,1,0:T(8,128)} copy(f32[1,8,64,256]{3,2,1,0:T(8,128)S(1)} %shard_map.28) | data formatting | bytes 1048576
Async XLA Ops:
  0.0 1.0 %copy-start = (f32[1,8,64,256]{3,2,1,0:T(8,128)S(1)}, f32[1,8,64,256]{3,2,1,0:T(8,128)}, u32[]{:S(2)}) copy-start(f32[1,8,64,256]{3,2,1,0:T(8,128)} %states.1) | copy-start | bytes 1572868
  1.0 1.0 %copy-start.1 = (f32[8,64,256]{2,1,0:T(8,128)S(1)}, f32[8,64,256]{2,1,0:T(8,128)}, u32[]{:S(2)}) copy-start(f32[8,64,256]{2,1,0:T(8,128)} %conduct.1) | copy-start | bytes 1572868

commit v4 on v3

--- a/solution.py
+++ b/solution.py
@@ -13,7 +13,6 @@
 PARTS = 2
 EDGE = 8
 MESH = pl.DeviceIdType.MESH
-HIGHEST = lax.Precision.HIGHEST
 
 
 def group_matrix(shape, dim):
@@ -23,8 +22,22 @@
     return jnp.where((first >= 0) & (first < coarsen), 1.0, 0.0).astype(jnp.float32)
 
 
-def dot(a, b):
-    return jnp.dot(a, b, precision=HIGHEST, preferred_element_type=jnp.float32)
+def terms(a):
+    parts = []
+    for _ in range(3):
+        parts.append(a.astype(jnp.bfloat16))
+        a = a - parts[-1].astype(jnp.float32)
+    return parts
+
+
+def dot_right(a, ones):
+    ones = ones.astype(jnp.bfloat16)
+    return sum(jnp.dot(t, ones, preferred_element_type=jnp.float32) for t in terms(a)[::-1])
+
+
+def dot_left(ones, b):
+    ones = ones.astype(jnp.bfloat16)
+    return sum(jnp.dot(ones, t, preferred_element_type=jnp.float32) for t in terms(b)[::-1])
 
 
 def kernel(
@@ -104,12 +117,13 @@
             device_id=(tm, me + step), device_id_type=MESH,
         )
 
-    def halo_c(side):
+    def halo_c(side, q):
         step = 1 if side == 0 else -1
+        at = pl.ds(q * part, part)
         return pltpu.make_async_remote_copy(
-            src_ref=conduct.at[planes - 1 if side == 0 else 0],
-            dst_ref=cond.at[0 if side == 0 else planes + 1],
-            send_sem=csend.at[side], recv_sem=crecv.at[side],
+            src_ref=conduct.at[planes - 1 if side == 0 else 0, at],
+            dst_ref=cond.at[0 if side == 0 else planes + 1, at],
+            send_sem=csend.at[side, q], recv_sem=crecv.at[side, q],
             device_id=(tm, me + step), device_id_type=MESH,
         )
 
@@ -119,8 +133,8 @@
     for side in range(2):
         @pl.when(sends_side[side])
         def _(side=side):
-            halo_c(side).start()
             for q in range(PARTS):
+                halo_c(side, q).start()
                 halo(0, side, q).start()
 
     lane = lax.broadcasted_iota(jnp.int32, (crows, LANES), 1)
@@ -134,8 +148,8 @@
             for j in range(1, coarsen):
                 total = total + ref[(*lead, 1 + c * coarsen + j)]
             sums.append(total)
-        lanes = dot(jnp.concatenate(sums, axis=0), gather_y)
-        return dot(gather_x, lanes) * (1.0 / coarsen**3)
+        lanes = dot_right(jnp.concatenate(sums, axis=0), gather_y)
+        return dot_left(gather_x, lanes) * (1.0 / coarsen**3)
 
     def packed(value):
         parts = []
@@ -179,7 +193,6 @@
             def _(d=d):
                 early(d).start()
 
-    early_send([d for d in offsets if abs(d) <= near])
 
     half = 0.5 * fine_rate
     row_face = lax.broadcasted_iota(jnp.int32, (rows, cols), 0) < rows - 1
@@ -239,14 +252,15 @@
 
                 @pl.when(hears_side[side])
                 def _(side=side):
-                    if k == 0 and q == 0:
-                        halo_c(side).wait_recv()
+                    if k == 0:
+                        halo_c(side, q).wait_recv()
                     halo(k, side, q).wait_recv()
 
-                if k == 0 and q == 0:
+                if k == 0:
                     low_plane = 0 if side == 0 else planes
                     scale = jnp.where(hears_side[side], half, 0.0)
-                    az[low_plane] = scale * (cond[low_plane] + cond[low_plane + 1])
+                    span = slice(q * part, (q + 1) * part)
+                    az[low_plane, span] = scale * (cond[low_plane, span] + cond[low_plane + 1, span])
                 advance_part(k, edge, q)
                 if k < FSTEPS - 1:
                     @pl.when(sends_side[1 - side])
@@ -303,7 +317,7 @@
             start_copy(delta).start()
 
     fine_step(0)
-    early_send([d for d in offsets if abs(d) > near])
+    early_send(offsets)
     if slices > 1:
         pass_token(0)
 
@@ -376,7 +390,7 @@
 
     spread_x = group_matrix((cplanes * rows, cplanes * crows), 1)
     spread_y = group_matrix((LANES, cols), 0)
-    spread = dot(dot(spread_x, change), spread_y)
+    spread = dot_right(dot_left(spread_x, change), spread_y)
     stores = []
     for c in range(cplanes):
         piece = spread[c * rows : (c + 1) * rows]
@@ -394,7 +408,8 @@
     for side in range(2):
         @pl.when(sends_side[side])
         def _(side=side):
-            halo_c(side).wait_send()
+            for q in range(PARTS):
+                halo_c(side, q).wait_send()
             for k in range(FSTEPS):
                 for q in range(PARTS):
                     halo(k, side, q).wait_send()
@@ -447,8 +462,8 @@
             dma((2 + cplanes,)),
             dma((FSTEPS, 2, PARTS)),
             dma((FSTEPS, 2, PARTS)),
-            dma((2,)),
-            dma((2,)),
+            dma((2, PARTS)),
+            dma((2, PARTS)),
             dma((blocks,)),
             dma((blocks,)),
             dma((hops,)),

time: 26.7 us -> 26.3 us (0.985); the launches traced: 26.5 us -> 25.8 us
  Pallas kernels: 23.7 us -> 22.9 us
    pallas_call x1, Pallas kernels: 23.7 us -> 22.9 us  [per_device(): pl.pallas_call(functools.partial(kernel, slices, slabs, reach), out_shape...]
where the time goes in v4:
time: 26.3 us; the launch traced here: 25.8 us
  Pallas kernels  22.9 us (87%)
  local copies, waits for them, and re-layouts  2.88 us (11%)
    pallas_call x1, Pallas kernels, per_device(): pl.pallas_call(functools.partial(kernel, slices, slabs, reach), out_shape...  22.9 us
    unnamed x5, local copies, waits for them, and re-layouts  2.88 us

profile of v4, /device:TPU:27, one launch (start us, length us, event | category | flops | bytes accessed | tf_op | source)
XLA Modules:
  0.0 25.8 jit_solution(4930419939195311748)
XLA Ops:
  0.0 0.0 copy-start
  0.0 1.0 %copy-done = f32[1,8,64,256]{3,2,1,0:T(8,128)S(1)} copy-done((f32[1,8,64,256]{3,2,1,0:T(8,128)S(1)}, f32[1,8,64,256]{3,2,1,0:T(8,128)}, u32[]{:S(2)}) %copy-start) | copy-done | bytes 524312
  1.0 0.0 copy-start.1
  1.0 1.0 %copy-done.1 = f32[8,64,256]{2,1,0:T(8,128)S(1)} copy-done((f32[8,64,256]{2,1,0:T(8,128)S(1)}, f32[8,64,256]{2,1,0:T(8,128)}, u32[]{:S(2)}) %copy-start.1) | copy-done | bytes 524312
  2.1 22.9 %shard_map.28 = f32[1,8,64,256]{3,2,1,0:T(8,128)S(1)} custom-call(f32[1,8,64,256]{3,2,1,0:T(8,128)S(1)} %copy-done, f32[8,64,256]{2,1,0:T(8,128)S(1)} %copy-done.1), custom_call_target="tpu_custom_call" | custom-call | tf_op jit(solution)/shard_map/pallas_call | solution.py:446
  25.0 0.8 %copy.4 = f32[1,8,64,256]{3,2,1,0:T(8,128)} copy(f32[1,8,64,256]{3,2,1,0:T(8,128)S(1)} %shard_map.28) | data formatting | bytes 1048576
Async XLA Ops:
  0.0 1.0 %copy-start = (f32[1,8,64,256]{3,2,1,0:T(8,128)S(1)}, f32[1,8,64,256]{3,2,1,0:T(8,128)}, u32[]{:S(2)}) copy-start(f32[1,8,64,256]{3,2,1,0:T(8,128)} %states.1) | copy-start | bytes 1572868
  1.0 1.0 %copy-start.1 = (f32[8,64,256]{2,1,0:T(8,128)S(1)}, f32[8,64,256]{2,1,0:T(8,128)}, u32[]{:S(2)}) copy-start(f32[8,64,256]{2,1,0:T(8,128)} %conduct.1) | copy-start | bytes 1572868
